TPU v7x, 32 devices: a whole 2x2x4 slice. The times are simulated.
32 devices in a mesh: dp: 16 (over z, x, core), tensor: 2 (over y).
Axes of the slice: x: 2, y: 2, z: 4, core: 2. Of those that a mesh axis runs over, the one named last changes fastest.
Arguments:
- tokens: bfloat16 [16384, 1024], P(('dp', 'tensor')), may hold values from -6 to 6
- ln1_gain: float32 [1024], replicated, may hold values from 0.5 to 1.5
- ln1_bias: float32 [1024], replicated, may hold values from -1.75 to 1.75
- w_qkv: bfloat16 [3, 1024, 1024], P(None, 'dp', 'tensor'), may hold values from -0.25 to 0.25
- qv_bias: float32 [2, 1024], replicated, may hold values from -3 to 3
- w_out: bfloat16 [1024, 1024], P('tensor', 'dp'), may hold values from -0.75 to 0.75
- out_bias: float32 [1024], replicated, may hold values from -1.75 to 1.75
- ln2_gain: float32 [1024], replicated, may hold values from 0.5 to 1.5
- ln2_bias: float32 [1024], replicated, may hold values from -1.75 to 1.75
- w_fc: bfloat16 [1024, 4096], P('dp', 'tensor'), may hold values from -0.1875 to 0.1875
- fc_bias: float32 [4096], replicated, may hold values from -3 to 3
- w_proj: bfloat16 [4096, 1024], P('tensor', 'dp'), may hold values from -0.125 to 0.125
- proj_bias: float32 [1024], replicated, may hold values from -1.75 to 1.75
- cotangent: bfloat16 [16384, 1024], P(('dp', 'tensor')), may hold values from -6 to 6
Outputs:
- block_out: bfloat16 [16384, 1024], P(('dp', 'tensor'))
- input_grad: bfloat16 [16384, 1024], P(('dp', 'tensor'))
- grad_ln1_gain: float32 [1024], replicated
- grad_ln1_bias: float32 [1024], replicated
- grad_qkv: float32 [3, 1024, 1024], P(None, 'dp', 'tensor')
- grad_qv_bias: float32 [2, 1024], replicated
- grad_out: float32 [1024, 1024], P('tensor', 'dp')
- grad_out_bias: float32 [1024], replicated
- grad_ln2_gain: float32 [1024], replicated
- grad_ln2_bias: float32 [1024], replicated
- grad_fc: float32 [1024, 4096], P('dp', 'tensor')
- grad_fc_bias: float32 [4096], replicated
- grad_proj: float32 [4096, 1024], P('tensor', 'dp')
- grad_proj_bias: float32 [1024], replicated
All inputs are finite; a program needn't handle non-finite values.
Results may differ from a plain program's by a relative error of at most 0.018.
Values may be sent and summed in bfloat16 or wider, within the bound.
A program may use at most 192 MiB of HBM per device.

v0:
```python
import math

import jax
import jax.numpy as jnp
from jax import lax
from jax.sharding import PartitionSpec as P

HD = 64
LEN = 1024
QBLK = 512


EPSILON = 1e-05


def norm_rows(rows_in, gain, shift):
    centre = jnp.mean(rows_in, axis=-1, keepdims=True)
    centred = rows_in - centre
    spread = jnp.mean(centred * centred, axis=-1, keepdims=True)
    return centred * lax.rsqrt(spread + EPSILON) * gain + shift


def gelu_tanh(pre_act):
    return jax.nn.gelu(pre_act, approximate=True)


def gather_rows(local_rows):
    return lax.all_gather(local_rows, "tensor", axis=0, tiled=True)


def spread_rows(row_term, tok_rows):
    return lax.psum_scatter(
        row_term(jnp.int32(0), tok_rows * lax.axis_size("tensor")),
        "tensor",
        scatter_dimension=0,
        tiled=True,
    )


def contract_rows(left_side, right_side):
    return lax.dot_general(
        left_side, right_side, (((0,), (0,)), ((), ())), preferred_element_type=jnp.float32
    )


def contract_cols(left_side, right_side):
    return lax.dot_general(
        left_side, right_side, (((1,), (1,)), ((), ())), preferred_element_type=jnp.float32
    )


def rows_times(left_side, right_side, flipped):

    def row_term(offset, length):
        if flipped:
            return contract_cols(left_side, right_side)
        return jnp.dot(left_side, right_side, preferred_element_type=jnp.float32)

    return row_term


def masked_scores(query_block, key_seq, block_start, score_scale):
    scores = (
        jnp.einsum("qhd,khd->hqk", query_block, key_seq, preferred_element_type=jnp.float32)
        * score_scale
    )
    query_pos = block_start + lax.broadcasted_iota(jnp.int32, (QBLK, LEN), 0)
    key_pos = lax.broadcasted_iota(jnp.int32, (QBLK, LEN), 1)
    return jnp.where((key_pos <= query_pos)[None], scores, -1e30)


def block_inputs(query_rows, key_rows, value_rows, block_index):
    per_seq = LEN // QBLK
    sequence = block_index // per_seq
    block_start = block_index % per_seq * QBLK
    query_block = lax.dynamic_slice_in_dim(query_rows, block_index * QBLK, QBLK, 0)
    key_seq = lax.dynamic_slice_in_dim(key_rows, sequence * LEN, LEN, 0)
    value_seq = lax.dynamic_slice_in_dim(value_rows, sequence * LEN, LEN, 0)
    return (sequence, block_start, query_block, key_seq, value_seq)


def attend_forward(query_rows, key_rows, value_rows, score_scale):
    block_count = query_rows.shape[0] // QBLK

    def one_block(block_index):
        sequence, block_start, query_block, key_seq, value_seq = block_inputs(
            query_rows, key_rows, value_rows, block_index
        )
        scores = masked_scores(query_block, key_seq, block_start, score_scale)
        row_top = jnp.max(scores, axis=-1, keepdims=True)
        weights = jnp.exp(scores - row_top)
        row_total = jnp.sum(weights, axis=-1, keepdims=True)
        weights_low = (weights / row_total).astype(jnp.bfloat16)
        attended = jnp.einsum(
            "hqk,khd->qhd", weights_low, value_seq, preferred_element_type=jnp.float32
        )
        return (attended.astype(jnp.bfloat16), row_top[..., 0] + jnp.log(row_total[..., 0]))

    return lax.map(one_block, jnp.arange(block_count, dtype=jnp.int32))


def attend_backward(query_rows, key_rows, value_rows, d_attended, log_totals, score_scale):
    block_count = query_rows.shape[0] // QBLK

    def one_block(running, block_index):
        d_key_rows, d_value_rows = running
        sequence, block_start, query_block, key_seq, value_seq = block_inputs(
            query_rows, key_rows, value_rows, block_index
        )
        d_block = lax.dynamic_slice_in_dim(d_attended, block_index * QBLK, QBLK, 0)
        scores = masked_scores(query_block, key_seq, block_start, score_scale)
        block_totals = lax.dynamic_index_in_dim(log_totals, block_index, 0, keepdims=False)
        weights = jnp.exp(scores - block_totals[..., None])
        d_weights = jnp.einsum(
            "qhd,khd->hqk", d_block, value_seq, preferred_element_type=jnp.float32
        )
        d_scores = weights * (d_weights - jnp.sum(weights * d_weights, axis=-1, keepdims=True))
        d_scores = d_scores.astype(jnp.bfloat16)
        d_query = (
            jnp.einsum("hqk,khd->qhd", d_scores, key_seq, preferred_element_type=jnp.float32)
            * score_scale
        )
        key_part = (
            jnp.einsum("hqk,qhd->khd", d_scores, query_block, preferred_element_type=jnp.float32)
            * score_scale
        )
        value_part = jnp.einsum(
            "hqk,qhd->khd",
            weights.astype(jnp.bfloat16),
            d_block,
            preferred_element_type=jnp.float32,
        )
        seq_start = sequence * LEN
        d_key_rows = lax.dynamic_update_slice_in_dim(
            d_key_rows,
            lax.dynamic_slice_in_dim(d_key_rows, seq_start, LEN, 0) + key_part,
            seq_start,
            0,
        )
        d_value_rows = lax.dynamic_update_slice_in_dim(
            d_value_rows,
            lax.dynamic_slice_in_dim(d_value_rows, seq_start, LEN, 0) + value_part,
            seq_start,
            0,
        )
        return ((d_key_rows, d_value_rows), d_query)

    zeros_rows = jnp.zeros(key_rows.shape, jnp.float32)
    (d_key_rows, d_value_rows), d_queries = lax.scan(
        one_block, (zeros_rows, zeros_rows), jnp.arange(block_count, dtype=jnp.int32)
    )
    return (d_queries, d_key_rows, d_value_rows)


def body(
    tokens,
    ln1_gain,
    ln1_bias,
    w_qkv,
    qv_bias,
    w_out,
    out_bias,
    ln2_gain,
    ln2_bias,
    w_fc,
    fc_bias,
    w_proj,
    proj_bias,
    cotangent,
):
    tok_rows = tokens.shape[0]
    tensor_rank = lax.axis_index("tensor")
    head_cols = w_qkv.shape[2]
    hidden_cols = w_fc.shape[1]
    local_heads = head_cols // HD
    score_scale = 1.0 / math.sqrt(HD)
    qkv_full, out_rows, fc_cols, proj_rows = (
        lax.all_gather(w_qkv, "dp", axis=1, tiled=True),
        lax.all_gather(w_out, "dp", axis=1, tiled=True),
        lax.all_gather(w_fc, "dp", axis=0, tiled=True),
        lax.all_gather(w_proj, "dp", axis=1, tiled=True),
    )
    bias_query = lax.dynamic_slice_in_dim(qv_bias, tensor_rank * head_cols, head_cols, 1)
    inputs = tokens.astype(jnp.float32)
    normed_one, norm_one_back = jax.vjp(norm_rows, inputs, ln1_gain, ln1_bias)
    seen_one = gather_rows(normed_one.astype(jnp.bfloat16))
    group_rows = seen_one.shape[0]
    projected = jnp.einsum("rd,kdc->krc", seen_one, qkv_full, preferred_element_type=jnp.float32)
    query_rows = (
        (projected[0] + bias_query[0]).astype(jnp.bfloat16).reshape(group_rows, local_heads, HD)
    )
    key_rows = projected[1].astype(jnp.bfloat16).reshape(group_rows, local_heads, HD)
    value_rows = (
        (projected[2] + bias_query[1]).astype(jnp.bfloat16).reshape(group_rows, local_heads, HD)
    )
    attended, log_totals = attend_forward(query_rows, key_rows, value_rows, score_scale)
    attended = attended.reshape(group_rows, head_cols)
    branch_one = spread_rows(rows_times(attended, out_rows, False), tok_rows)
    hidden_res = inputs + (branch_one + out_bias)
    normed_two, norm_two_back = jax.vjp(norm_rows, hidden_res, ln2_gain, ln2_bias)
    normed_two = normed_two.astype(jnp.bfloat16)
    bias_hidden = lax.dynamic_slice_in_dim(fc_bias, tensor_rank * hidden_cols, hidden_cols, 0)
    seen_two = gather_rows(normed_two)
    pre_act = jnp.dot(seen_two, fc_cols, preferred_element_type=jnp.float32) + bias_hidden
    activated, gelu_back = jax.vjp(gelu_tanh, pre_act)
    activated = activated.astype(jnp.bfloat16)
    branch_two = spread_rows(rows_times(activated, proj_rows, False), tok_rows)
    block_out = (hidden_res + (branch_two + proj_bias)).astype(jnp.bfloat16)
    grad_final = cotangent.astype(jnp.float32)
    grad_proj_bias = jnp.sum(grad_final, axis=0)
    seen_grad = gather_rows(cotangent)
    d_proj_local = contract_rows(activated, seen_grad)
    d_pre = gelu_back(contract_cols(seen_grad, proj_rows))[0].astype(jnp.bfloat16)
    local_bias_grad = jnp.sum(d_pre, axis=0, dtype=jnp.float32)
    grad_fc_bias = lax.dynamic_update_slice_in_dim(
        jnp.zeros(fc_bias.shape, jnp.float32), local_bias_grad, tensor_rank * hidden_cols, 0
    )
    d_fc_local = contract_rows(seen_two, d_pre)
    d_normed_two = spread_rows(rows_times(d_pre, fc_cols, True), tok_rows)
    d_hidden_norm, grad_ln2_gain, grad_ln2_bias = norm_two_back(d_normed_two)
    grad_hidden = grad_final + d_hidden_norm
    grad_hidden_low = grad_hidden.astype(jnp.bfloat16)
    grad_out_bias = jnp.sum(grad_hidden_low, axis=0, dtype=jnp.float32)
    seen_hidden = gather_rows(grad_hidden_low)
    d_out_local = contract_rows(attended, seen_hidden)
    d_attended = contract_cols(seen_hidden, out_rows).astype(jnp.bfloat16)
    d_queries, d_key_rows, d_value_rows = attend_backward(
        query_rows,
        key_rows,
        value_rows,
        d_attended.reshape(group_rows, local_heads, HD),
        log_totals,
        score_scale,
    )
    stacked = jnp.stack(
        [
            d_queries.reshape(group_rows, head_cols).astype(jnp.bfloat16),
            d_key_rows.reshape(group_rows, head_cols).astype(jnp.bfloat16),
            d_value_rows.reshape(group_rows, head_cols).astype(jnp.bfloat16),
        ]
    )
    d_qkv = jnp.einsum("rd,krc->kdc", seen_one, stacked, preferred_element_type=jnp.float32)
    local_qv = jnp.stack(
        [
            jnp.sum(stacked[0], axis=0, dtype=jnp.float32),
            jnp.sum(stacked[2], axis=0, dtype=jnp.float32),
        ]
    )
    grad_qv_bias = lax.dynamic_update_slice_in_dim(
        jnp.zeros(qv_bias.shape, jnp.float32), local_qv, tensor_rank * head_cols, 1
    )

    def qkv_term(offset, length):
        return jnp.einsum("krc,kdc->rd", stacked, qkv_full, preferred_element_type=jnp.float32)

    d_normed_one = spread_rows(qkv_term, tok_rows)
    d_inputs_norm, grad_ln1_gain, grad_ln1_bias = norm_one_back(d_normed_one)
    input_grad = (grad_hidden + d_inputs_norm).astype(jnp.bfloat16)
    grad_qkv, grad_out, grad_fc, grad_proj = (
        lax.psum_scatter(d_qkv.astype(jnp.bfloat16), "dp", scatter_dimension=1, tiled=True).astype(
            jnp.float32
        ),
        lax.psum_scatter(
            d_out_local.astype(jnp.bfloat16), "dp", scatter_dimension=1, tiled=True
        ).astype(jnp.float32),
        lax.psum_scatter(
            d_fc_local.astype(jnp.bfloat16), "dp", scatter_dimension=0, tiled=True
        ).astype(jnp.float32),
        lax.psum_scatter(
            d_proj_local.astype(jnp.bfloat16), "dp", scatter_dimension=1, tiled=True
        ).astype(jnp.float32),
    )
    summed = lax.psum(
        (
            grad_ln1_gain,
            grad_ln1_bias,
            grad_qv_bias,
            grad_out_bias,
            grad_ln2_gain,
            grad_ln2_bias,
            grad_fc_bias,
            grad_proj_bias,
        ),
        ("dp", "tensor"),
    )
    return (
        block_out,
        input_grad,
        summed[0],
        summed[1],
        grad_qkv,
        summed[2],
        grad_out,
        summed[3],
        summed[4],
        summed[5],
        grad_fc,
        summed[6],
        grad_proj,
        summed[7],
    )


def solution(mesh):
    in_specs = (
        P(("dp", "tensor"), None),
        P(),
        P(),
        P(None, "dp", "tensor"),
        P(),
        P("tensor", "dp"),
        P(),
        P(),
        P(),
        P("dp", "tensor"),
        P(),
        P("tensor", "dp"),
        P(),
        P(("dp", "tensor"), None),
    )
    out_specs = (
        P(("dp", "tensor"), None),
        P(("dp", "tensor"), None),
        P(),
        P(),
        P(None, "dp", "tensor"),
        P(),
        P("tensor", "dp"),
        P(),
        P(),
        P(),
        P("dp", "tensor"),
        P(),
        P("tensor", "dp"),
        P(),
    )
    return jax.shard_map(body, mesh=mesh, in_specs=in_specs, out_specs=out_specs, check_vma=False)
```

profile of v0, /device:TPU:0, one launch (start us, length us, event | category | flops | bytes accessed | tf_op | source)
XLA Modules:
  0.0 981.3 jit_solution(116231164404986343)
XLA Ops:
  8.7 1.6 fusion.42
  10.4 2.7 fusion.40
  14.9 34.2 %all-gather.9.cloned.1.call-done = bf16[1024,1024]{1,0:T(8,128)(2,1)} async-done(((bf16[512,1024]{1,0:T(8,128)(2,1)}), bf16[1024,1024]{1,0:T(8,128)(2,1)}) %all-gather.9.cloned.1.call-update) | async-done | bytes 2097168 | tf_op jit(solution)/shard_map/all_gather | solution.py:28
  49.0 47.4 %all-gather.11.cloned.1.call-done = bf16[3,1024,512]{2,1,0:T(8,128)(2,1)} async-done(((bf16[3,64,512]{2,1,0:T(8,128)(2,1)}), bf16[3,1024,512]{2,1,0:T(8,128)(2,1)}) %all-gather.11.cloned.1.call-update) | async-done | bytes 3145744 | tf_op jit(solution)/shard_map/all_gather | solution.py:178
  96.5 6.2 convolution_bitcast_fusion
  104.3 34.8 %while.31 = (s32[]{:T(128)}, bf16[2,512,8,64]{1,3,2,0:T(8,128)(2,1)S(1)}, f32[2,8,512]{2,1,0:T(8,128)S(1)}, s32[2]{0:T(128)S(1)}, bf16[1024,8,64]{0,2,1:T(8,128)...) while((s32[]{:T(128)}, ...), condition=%wide.region_5.6_spmd, body=%wide.region_2.5_spmd.sunk | while | flops 1124856320 | bytes 55710016 | solution.py:99
  108.1 4.1 fusion.105
  112.2 4.2 fusion.106
  116.4 5.4 fusion.107
  125.4 4.1 fusion.105
  129.5 4.2 fusion.106
  133.8 5.4 fusion.107
  141.5 4.5 fusion.59
  146.6 52.6 %reduce-scatter.8.cloned.1.call-done = f32[512,1024]{1,0:T(8,128)} async-done(((f32[1024,1024]{1,0:T(8,128)}), f32[512,1024]{1,0:T(8,128)}) %reduce-scatter.8.cloned.1.call-update) | async-done | bytes 2097168 | tf_op jit(solution)/shard_map/reduce_scatter | solution.py:32
  199.3 1.9 fusion.57
  205.9 46.3 %all-gather.17.cloned.1.call-done = bf16[1024,2048]{1,0:T(8,128)(2,1)} async-done(((bf16[64,2048]{1,0:T(8,128)(2,1)}), bf16[1024,2048]{1,0:T(8,128)(2,1)}) %all-gather.17.cloned.1.call-update) | async-done | bytes 4194320 | tf_op jit(solution)/shard_map/all_gather | solution.py:180
  252.2 33.7 %all-gather.15.cloned.1.call-done = bf16[1024,1024]{1,0:T(8,128)(2,1)} async-done(((bf16[512,1024]{1,0:T(8,128)(2,1)}), bf16[1024,1024]{1,0:T(8,128)(2,1)}) %all-gather.15.cloned.1.call-update) | async-done | bytes 2097168 | tf_op jit(solution)/shard_map/all_gather | solution.py:28
  285.9 10.9 %fusion.60 = f32[1024,2048]{1,0:T(8,128)} fusion(bf16[1024,1024]{1,0:T(8,128)(2,1)} %all-gather.15.cloned.1.call-done, bf16[1024,2048]{1,0:T(8,128)(2,1)} %all-gather.17.cloned.1.call-done), kind=kOutput, calls=%fused_computation.114 | convolution fusion | flops 4294967296 | bytes 14680064 | tf_op jit(solution)/shard_map/dot_general | solution.py:204
  296.8 23.9 %all-gather.21.cloned.1.call-done = bf16[1024,1024]{1,0:T(8,128)(2,1)} async-done(((bf16[512,1024]{1,0:T(8,128)(2,1)}), bf16[1024,1024]{1,0:T(8,128)(2,1)}) %all-gather.21.cloned.1.call-update) | async-done | bytes 2097168 | tf_op jit(solution)/shard_map/all_gather | solution.py:28
  320.7 53.0 %all-gather.19.cloned.1.call-done = bf16[2048,1024]{0,1:T(8,128)(2,1)} async-done(((bf16[2048,64]{0,1:T(8,128)(2,1)}), bf16[2048,1024]{0,1:T(8,128)(2,1)}) %all-gather.19.cloned.1.call-update) | async-done | bytes 4194320 | tf_op jit(solution)/shard_map/all_gather | solution.py:181
  373.7 13.7 %convert_reduce_fusion = (f32[2048]{0:T(1024)}, bf16[1024,2048]{1,0:T(8,128)(2,1)S(1)}) fusion(f32[1024,2048]{1,0:T(8,128)} %fusion.60, f32[2048]{0:T(1024)S(1)} %dynamic_slice.51, bf16[1024,1024]{1,0:T(8,128)(2,1)} %all-gather.21.cloned.1.call-done, bf16[2048,1024]{0,1:T(8,128)(2,1)} %all-gather.19.cloned.1.call-done), kind=kOutput, calls=%fused_computation.48 | convolution fusion | flops 4343199744 | bytes 18890752 | tf_op jit(solution)/shard_map/dot_general | solution.py:47
  387.4 2.1 copy-done.46
  389.5 6.1 fusion.61
  395.8 12.1 %fusion.52 = f32[1024,1024]{1,0:T(8,128)} fusion(bf16[2048,1024]{0,1:T(8,128)(2,1)} %all-gather.19.cloned.1.call-done, f32[1024,2048]{1,0:T(8,128)} %fusion.60, f32[2048]{0:T(1024)S(1)} %dynamic_slice.51), kind=kOutput, calls=%fused_computation.108 | convolution fusion | flops 4315938816 | bytes 16785408 | tf_op jit(solution)/shard_map/dot_general | solution.py:57
  408.1 40.5 %reduce-scatter.12.cloned.1.call-done = f32[512,1024]{1,0:T(8,128)} async-done(((f32[1024,1024]{1,0:T(8,128)}), f32[512,1024]{1,0:T(8,128)}) %reduce-scatter.12.cloned.1.call-update) | async-done | bytes 2097168 | tf_op jit(solution)/shard_map/reduce_scatter | solution.py:32
  448.6 3.6 multiply_reduce_fusion.1
  452.2 52.9 %reduce-scatter.10.cloned.1.call-done = f32[512,1024]{1,0:T(8,128)} async-done(((f32[1024,1024]{1,0:T(8,128)}), f32[512,1024]{1,0:T(8,128)}) %reduce-scatter.10.cloned.1.call-update) | async-done | bytes 2097168 | tf_op jit(solution)/shard_map/reduce_scatter | solution.py:32
  505.0 4.6 fusion.56
  511.0 1.9 convert_reduce_fusion.3
  513.0 10.8 %convolution_convert_fusion = bf16[2048,1024]{0,1:T(8,128)(2,1)} fusion(bf16[1024,1024]{1,0:T(8,128)(2,1)} %all-gather.21.cloned.1.call-done, f32[1024,2048]{1,0:T(8,128)} %fusion.60, f32[2048]{0:T(1024)S(1)} %dynamic_slice.51), kind=kOutput, calls=%fused_computation.50 | convolution fusion | flops 4318035968 | bytes 14688256 | tf_op jit(solution)/shard_map/dot_general | solution.py:41
  524.0 9.3 convolution_convert_fusion.1
  533.4 12.9 %all-gather.23.cloned.1.call-done = bf16[1024,1024]{1,0:T(8,128)(2,1)} async-done(((bf16[512,1024]{1,0:T(8,128)(2,1)}), bf16[1024,1024]{1,0:T(8,128)(2,1)}) %all-gather.23.cloned.1.call-update) | async-done | bytes 2097168 | tf_op jit(solution)/shard_map/all_gather | solution.py:28
  546.3 3.9 convolution_convert_fusion.3
  550.1 97.1 %while.32 = (s32[]{:T(128)}, f32[1024,8,64]{0,2,1:T(8,128)}, f32[1024,8,64]{0,2,1:T(8,128)}, bf16[2,512,8,64]{1,3,2,0:T(8,128)(2,1)}, s32[2]{0:T(128)S(1)}, /*in...) while((s32[]{:T(128)}, f32[1024,8,64]{0,2,1:T(8,128)}, ...), condition=%wide.region_15.16_spmd.clone, body=%wide.region_13.15_spmd.clone.sunk | while | flops 2725507584 | bytes 213209776 | solution.py:149
  556.9 3.8 fusion.117
  560.8 11.5 %multiply_reduce_fusion.5 = (f32[8,512]{1,0:T(8,128)}, f32[8,512,1024]{2,1,0:T(8,128)}) fusion(f32[8,512,1024]{2,1,0:T(8,128)S(1)} %fusion.117, f32[8,512]{1,0:T(8,128)} %dynamic-slice_bitcast_fusion.2, bf16[1024,8,64]{0,2,1:T(8,128)(2,1)S(1)} %get-tuple-element.569, bf16[1024,8,64]{0,2,1:T(8,128)(2,1)} %get-tuple-element.568, s32[]{:T(128)S(6)} %select_n.109, ...), kind=kOutput, calls=%fused_computation.18.clone.1 | convolution fusion | flops 557838336 | bytes 35684356 | tf_op jit(solution)/shard_map/while/body/eval_jaxpr/qhd,khd->hqk/dot_general | solution.py:64
  572.3 9.4 multiply_convert_fusion.5
  581.7 8.9 bitcast_add_fusion.5
  590.6 2.7 fusion.118
  593.3 3.2 bitcast_add_fusion.4
  604.3 3.8 fusion.117
  608.1 11.4 %multiply_reduce_fusion.5 = (f32[8,512]{1,0:T(8,128)}, f32[8,512,1024]{2,1,0:T(8,128)}) fusion(f32[8,512,1024]{2,1,0:T(8,128)S(1)} %fusion.117, f32[8,512]{1,0:T(8,128)} %dynamic-slice_bitcast_fusion.2, bf16[1024,8,64]{0,2,1:T(8,128)(2,1)S(1)} %get-tuple-element.569, bf16[1024,8,64]{0,2,1:T(8,128)(2,1)} %get-tuple-element.568, s32[]{:T(128)S(6)} %select_n.109, ...), kind=kOutput, calls=%fused_computation.18.clone.1 | convolution fusion | flops 557838336 | bytes 35684356 | tf_op jit(solution)/shard_map/while/body/eval_jaxpr/qhd,khd->hqk/dot_general | solution.py:64
  619.5 9.4 multiply_convert_fusion.5
  629.0 10.2 %bitcast_add_fusion.5 = f32[1024,8,64]{0,2,1:T(8,128)} fusion(f32[1024,8,64]{0,2,1:T(8,128)} %get-tuple-element.550, f32[8,512,1024]{2,1,0:T(8,128)} %get-tuple-element.495, pred[]{:T(512)S(6)} %compare.9, bf16[1024,8,64]{0,2,1:T(8,128)(2,1)S(1)} %copy-done.8, s32[]{:T(128)S(6)} %select_n.109), kind=kOutput, calls=%fused_computation.22.clone.1 | convolution fusion | flops 542113792 | bytes 21495812 | tf_op jit(solution)/shard_map/while/body/eval_jaxpr/hqk,qhd->khd/dot_general | solution.py:127
  639.8 2.7 fusion.118
  642.5 3.3 bitcast_add_fusion.4
  647.2 1.8 convert_element_type.166
  650.4 1.7 copy.49
  652.1 2.2 reshape.215
  654.3 2.4 convert_reduce_fusion.4
  658.1 7.2 convert_bitcast_fusion
  665.2 7.6 copy.46
  674.1 3.9 convolution_convert_fusion.2
  678.1 7.6 convolution_bitcast_fusion.1
  688.0 1.8 convert_element_type.183
  689.7 8.5 reduce-scatter.18.cloned.1.call-done
  698.2 1.8 convert_element_type.180
  700.4 112.6 %all-reduce.4.cloned.1.call-done = bf16[3,1024,512]{2,0,1:T(4,128)(2,1)} async-done(((bf16[3,1024,512]{2,0,1:T(4,128)(2,1)}), bf16[3,1024,512]{2,0,1:T(4,128)(2,1)}) %all-reduce.4.cloned.1.call-update) | async-done | bytes 3145744
  814.8 57.9 %reduce-scatter.16.cloned.1.call-done = bf16[512,64]{0,1:T(8,128)(2,1)} async-done(((bf16[512,1024]{0,1:T(8,128)(2,1)}), bf16[512,64]{0,1:T(8,128)(2,1)}) %reduce-scatter.16.cloned.1.call-update) | async-done | bytes 65552 | tf_op jit(solution)/shard_map/reduce_scatter | solution.py:263
  872.7 1.5 convert_element_type.177
  874.2 54.1 %reduce-scatter.14.cloned.1.call-done = f32[512,1024]{1,0:T(8,128)} async-done(((f32[1024,1024]{1,0:T(8,128)}), f32[512,1024]{1,0:T(8,128)}) %reduce-scatter.14.cloned.1.call-update) | async-done | bytes 2097168 | tf_op jit(solution)/shard_map/reduce_scatter | solution.py:32
  928.4 2.3 fusion.53
  931.8 2.0 convert_reduce_fusion.2
  933.8 40.8 %all-reduce.1 = (f32[1024]{0:T(1024)}, f32[1024]{0:T(1024)}, f32[2,1024]{1,0:T(2,128)}, f32[1024]{0:T(1024)}, f32[1024]{0:T(1024)}, /*index=5*/f32[1024]{0:T(1024)}, f32[4096]{0:T(1024)}, f32[1024]{0:T(1024)}) all-reduce(f32[1024]{0:T(1024)S(1)} %get-tuple-element.315, ...), channel_id=1, replica_groups=mesh['dp'=16,'tensor'=2] {'dp','tensor'}, use_global_device_ids=true, to_apply=%region_20.21 | all-reduce | flops 12288 | bytes 98304 | tf_op jit(solution)/shard_map/psum | solution.py:273
  (203 shorter events, 33.6 us)
Async XLA Ops:
  7.2 7.4 copy-start.42
  7.2 41.8 %all-gather.9.cloned.1.call-start = ((), (), s32[]{:S(2)}) async-start(), calls=%async_computation.7 | async-start | bytes 3145728 | tf_op jit(solution)/shard_map/all_gather | solution.py:28
  8.7 87.8 %copy-start.24 = (f32[512]{0:T(512)}, f32[512]{0:T(512)S(1)}, u32[]{:S(2)}) copy-start(f32[512]{0:T(512)S(1)} %broadcast_multiply_fusion.1) | copy-start | bytes 6148
  10.3 86.1 %copy-start.30 = (f32[512]{0:T(512)}, f32[512]{0:T(512)S(1)}, u32[]{:S(2)}) copy-start(f32[512]{0:T(512)S(1)} %fusion.42) | copy-start | bytes 6148
  10.3 86.1 %copy-start.28 = (f32[512]{0:T(512)}, f32[512]{0:T(512)S(1)}, u32[]{:S(2)}) copy-start(f32[512]{0:T(512)S(1)} %fusion.47) | copy-start | bytes 6148
  13.0 83.4 %all-gather.11.cloned.1.call-start = ((), (), s32[]{:S(2)}) async-start(), calls=%async_computation.8 | async-start | bytes 3342336 | tf_op jit(solution)/shard_map/all_gather | solution.py:178
  13.8 126.7 %all-gather.13.cloned.1.call-start = ((), (), s32[]{:S(2)}) async-start(), calls=%async_computation.9 | async-start | bytes 1114112 | tf_op jit(solution)/shard_map/all_gather | solution.py:179
  14.5 184.7 %reduce-scatter.8.cloned.1.call-start = ((), (), s32[]{:S(2)}) async-start(), calls=%async_computation.10 | async-start | bytes 6291456 | tf_op jit(solution)/shard_map/reduce_scatter | solution.py:32
  146.0 53.3 %copy-start.6 = (bf16[512,1024]{1,0:T(8,128)(2,1)S(1)}, bf16[512,1024]{1,0:T(8,128)(2,1)}, u32[]{:S(2)}) copy-start(bf16[512,1024]{1,0:T(8,128)(2,1)} %param.18) | copy-start | bytes 3145732
  146.0 53.3 %copy-start.41 = (f32[1024]{0:T(1024)S(1)}, f32[1024]{0:T(1024)}, u32[]{:S(2)}) copy-start(f32[1024]{0:T(1024)} %param.24) | copy-start | bytes 12292
  146.0 106.2 %all-gather.17.cloned.1.call-start = ((), (), s32[]{:S(2)}) async-start(), calls=%async_computation.12 | async-start | bytes 4456448 | tf_op jit(solution)/shard_map/all_gather | solution.py:180
  146.6 56.0 %copy-start.27 = (f32[1024]{0:T(1024)S(1)}, f32[1024]{0:T(1024)}, u32[]{:S(2)}) copy-start(f32[1024]{0:T(1024)} %param.25) | copy-start | bytes 12292
  146.6 56.0 %copy-start.38 = (f32[1024]{0:T(1024)S(1)}, f32[1024]{0:T(1024)}, u32[]{:S(2)}) copy-start(f32[1024]{0:T(1024)} %param.26) | copy-start | bytes 12292
  146.6 139.3 %all-gather.15.cloned.1.call-start = ((), (), s32[]{:S(2)}) async-start(), calls=%async_computation.11 | async-start | bytes 3145728 | tf_op jit(solution)/shard_map/all_gather | solution.py:28
  201.6 4.4 copy-start.40
  204.0 116.7 %all-gather.21.cloned.1.call-start = ((), (), s32[]{:S(2)}) async-start(), calls=%async_computation.15 | async-start | bytes 3145728 | tf_op jit(solution)/shard_map/all_gather | solution.py:28
  204.7 169.0 %all-gather.19.cloned.1.call-start = ((), (), s32[]{:S(2)}) async-start(), calls=%async_computation.13 | async-start | bytes 4456448 | tf_op jit(solution)/shard_map/all_gather | solution.py:181
  205.5 243.1 %reduce-scatter.12.cloned.1.call-start = ((), (), s32[]{:S(2)}) async-start(), calls=%async_computation.16 | async-start | bytes 6291456 | tf_op jit(solution)/shard_map/reduce_scatter | solution.py:32
  373.7 15.8 %copy-start.43 = (bf16[1024,2048]{1,0:T(8,128)(2,1)S(1)}, bf16[1024,2048]{1,0:T(8,128)(2,1)}, u32[]{:S(2)}) copy-start(bf16[1024,2048]{1,0:T(8,128)(2,1)} %all-gather.17.cloned.1.call-done) | copy-start | bytes 12582916
  387.4 2.1 copy-start.46
  395.6 109.4 %reduce-scatter.10.cloned.1.call-start = ((), (), s32[]{:S(2)}) async-start(), calls=%async_computation.14 | async-start | bytes 6291456 | tf_op jit(solution)/shard_map/reduce_scatter | solution.py:32
  408.0 97.0 %copy-start.39 = (f32[1024]{0:T(1024)S(1)}, f32[1024]{0:T(1024)}, u32[]{:S(2)}) copy-start(f32[1024]{0:T(1024)} %param.30) | copy-start | bytes 12292
  408.0 138.3 %all-gather.23.cloned.1.call-start = ((), (), s32[]{:S(2)}) async-start(), calls=%async_computation.17 | async-start | bytes 3145728 | tf_op jit(solution)/shard_map/all_gather | solution.py:28
  452.1 58.9 %copy-start.12 = (bf16[512,1024]{1,0:T(8,128)(2,1)S(1)}, bf16[512,1024]{1,0:T(8,128)(2,1)}, u32[]{:S(2)}) copy-start(bf16[512,1024]{1,0:T(8,128)(2,1)} %param.31) | copy-start | bytes 3145732
  509.7 3.3 copy-start.32
  513.0 175.0 %reduce-scatter.20.cloned.1.call-start = ((), (), s32[]{:S(2)}) async-start(), calls=%async_computation.21 | async-start | bytes 4456448 | tf_op jit(solution)/shard_map/reduce_scatter | solution.py:269
  523.9 174.3 %reduce-scatter.18.cloned.1.call-start = ((), (), s32[]{:S(2)}) async-start(), calls=%async_computation.20 | async-start | bytes 4456448 | tf_op jit(solution)/shard_map/reduce_scatter | solution.py:266
  533.3 13.0 %copy-start.44 = (bf16[512,1024]{0,1:T(8,128)(2,1)S(1)}, bf16[512,1024]{0,1:T(8,128)(2,1)}, u32[]{:S(2)}) copy-start(bf16[512,1024]{0,1:T(8,128)(2,1)} %all-gather.13.cloned.1.call-done) | copy-start | bytes 3145732
  533.3 279.6 %all-reduce.4.cloned.1.call-start = ((), (), s32[]{:S(2)}) async-start(), calls=%async_computation.22 | async-start | bytes 8388608
  550.5 5.2 copy-start.3
  550.5 5.2 copy-start.22
  572.3 9.4 copy-start.8
  581.7 8.9 copy-start
  581.7 8.9 copy-start.14
  590.6 2.7 copy-start.1
  593.2 3.3 copy-start.15
  593.3 4.7 copy-start.4
  593.3 4.7 copy-start.23
  597.9 5.2 copy-start.3
  597.9 5.2 copy-start.22
  619.5 9.4 copy-start.8
  629.0 10.2 %copy-start = (bf16[8,512,1024]{2,1,0:T(8,128)(2,1)S(1)}, bf16[8,512,1024]{2,1,0:T(8,128)(2,1)}, u32[]{:S(2)}) copy-start(bf16[8,512,1024]{2,1,0:T(8,128)(2,1)} %multiply_convert_fusion.5) | copy-start | bytes 25165828 | tf_op jit(solution)/shard_map/while
  629.0 10.8 %copy-start.14 = (bf16[2,512,8,64]{1,3,2,0:T(8,128)(2,1)S(1)}, bf16[2,512,8,64]{1,3,2,0:T(8,128)(2,1)}, u32[]{:S(2)}) copy-start(bf16[2,512,8,64]{1,3,2,0:T(8,128)(2,1)} %get-tuple-element.551) | copy-start | bytes 3145732 | tf_op jit(solution)/shard_map/while
  639.8 2.7 copy-start.1
  642.5 3.3 copy-start.15
  642.5 4.7 copy-start.4
  642.5 4.7 copy-start.23
  647.2 3.2 copy-start.16
  654.3 3.8 copy-start.18
  654.3 3.8 copy-start.21
  672.9 199.8 %reduce-scatter.16.cloned.1.call-start = ((), (), s32[]{:S(2)}) async-start(), calls=%async_computation.19 | async-start | bytes 1114112 | tf_op jit(solution)/shard_map/reduce_scatter | solution.py:263
  678.0 250.3 %reduce-scatter.14.cloned.1.call-start = ((), (), s32[]{:S(2)}) async-start(), calls=%async_computation.18 | async-start | bytes 6291456 | tf_op jit(solution)/shard_map/reduce_scatter | solution.py:32
  685.7 14.3 %copy-start.17 = (bf16[2,512,8,64]{1,3,2,0:T(8,128)(2,1)S(1)}, bf16[2,512,8,64]{1,3,2,0:T(8,128)(2,1)}, u32[]{:S(2)}) copy-start(bf16[2,512,8,64]{1,3,2,0:T(8,128)(2,1)} %get-tuple-element.235) | copy-start | bytes 3145732
  685.7 242.6 %copy-start.7 = (bf16[512,1024]{1,0:T(8,128)(2,1)S(1)}, bf16[512,1024]{1,0:T(8,128)(2,1)}, u32[]{:S(2)}) copy-start(bf16[512,1024]{1,0:T(8,128)(2,1)} %param.18) | copy-start | bytes 3145732
  685.8 242.6 %copy-start.25 = (f32[512]{0:T(512)S(1)}, f32[512]{0:T(512)}, u32[]{:S(2)}) copy-start(f32[512]{0:T(512)} %copy-done.24) | copy-start | bytes 6148
  685.8 242.6 %copy-start.26 = (f32[1024]{0:T(1024)S(1)}, f32[1024]{0:T(1024)}, u32[]{:S(2)}) copy-start(f32[1024]{0:T(1024)} %param.19) | copy-start | bytes 12292
  700.0 230.7 %copy-start.31 = (f32[512]{0:T(512)S(1)}, f32[512]{0:T(512)}, u32[]{:S(2)}) copy-start(f32[512]{0:T(512)} %copy-done.30) | copy-start | bytes 6148
  700.0 230.7 %copy-start.29 = (f32[512]{0:T(512)S(1)}, f32[512]{0:T(512)}, u32[]{:S(2)}) copy-start(f32[512]{0:T(512)} %copy-done.28) | copy-start | bytes 6148
  874.2 57.5 %copy-start.13 = (bf16[512,1024]{1,0:T(8,128)(2,1)S(1)}, bf16[512,1024]{1,0:T(8,128)(2,1)}, u32[]{:S(2)}) copy-start(bf16[512,1024]{1,0:T(8,128)(2,1)} %param.31) | copy-start | bytes 3145732
  874.2 57.5 %copy-start.33 = (f32[512]{0:T(512)S(1)}, f32[512]{0:T(512)}, u32[]{:S(2)}) copy-start(f32[512]{0:T(512)} %copy-done.32) | copy-start | bytes 6148
  928.4 2.3 copy-start.9
  928.4 3.4 copy-start.11
  931.8 2.1 copy-start.34
  931.8 2.0 copy-start.35
  (9 other events, 12.3 us)
Sparse Core Ops, SparseCore 0:
  13.2 35.8 all-gather.8
  51.2 45.1 all-gather.10
  98.6 36.7 all-gather.12
  146.1 53.1 reduce-scatter.7
  201.5 50.6 all-gather.16
  254.3 31.6 all-gather.14
  287.5 33.1 all-gather.20
  323.1 50.5 all-gather.18
  395.7 52.7 reduce-scatter.11
  450.7 54.2 reduce-scatter.9
  513.1 33.1 all-gather.22
  550.5 72.4 reduce-scatter.19
  626.8 71.3 reduce-scatter.17
  702.2 110.7 all-reduce.3
  816.4 56.2 reduce-scatter.15
  875.0 53.3 reduce-scatter.13
where the time goes:
time: 987 us; the launch traced here: 981 us
  waiting for transfers between devices  634 us (64%)
  matrix products  177 us (18%)
  other arithmetic  67.1 us (7%)
  blocking collectives  40.8 us (4%)
  local copies, waits for them, and re-layouts  32.7 us (3%)
  between operations  15.3 us (2%)
  loops' own time  13.8 us (1%)
    reduce_scatter x4, waiting for transfers between devices, spread_rows(): lax.psum_scatter(row_term(jnp.int32(0), tok_rows * lax.axis_size('tensor'...  200 us
    unnamed x17, waiting for transfers between devices  116 us
    all_gather x4, waiting for transfers between devices, gather_rows(): return lax.all_gather(local_rows, 'tensor', axis=0, tiled=True)  105 us
    reduce_scatter x1, waiting for transfers between devices, body(): lax.psum_scatter(d_out_local.astype(jnp.bfloat16), 'dp', scatter_dimensio...  57.9 us
    all_gather x1, waiting for transfers between devices, body(): lax.all_gather(w_proj, 'dp', axis=1, tiled=True)  53 us
    all_gather x1, waiting for transfers between devices, body(): lax.all_gather(w_qkv, 'dp', axis=1, tiled=True)  47.4 us
    all_gather x1, waiting for transfers between devices, body(): lax.all_gather(w_fc, 'dp', axis=0, tiled=True)  46.3 us
    psum x1, blocking collectives, body(): lax.psum((grad_ln1_gain, grad_ln1_bias, grad_qv_bias, grad_out_bias, grad...  40.8 us
  transfers between devices with their start and end apart: 16, of which 14 were waited for; matrix products, arithmetic and copies ran while one was open for 23% of the time, Pallas kernels for 0%

commit v1 on v0

v1 whole, which is shorter than its diff:
```python
import math

import jax
import jax.numpy as jnp
from jax import lax
from jax.experimental import pallas as pl
from jax.experimental.pallas import tpu as pltpu
from jax.sharding import PartitionSpec as P

HD = 64
LEN = 1024
QB = 256
LANES = 128


EPSILON = 1e-05


def norm_rows(rows_in, gain, shift):
    centre = jnp.mean(rows_in, axis=-1, keepdims=True)
    centred = rows_in - centre
    spread = jnp.mean(centred * centred, axis=-1, keepdims=True)
    return centred * lax.rsqrt(spread + EPSILON) * gain + shift


def gelu_tanh(pre_act):
    return jax.nn.gelu(pre_act, approximate=True)


def shift_by(values, step):
    size = lax.axis_size("tensor")
    return lax.ppermute(values, "tensor", [(i, (i + step) % size) for i in range(size)])


def gather_rows(local_rows):
    size = lax.axis_size("tensor")
    rank = lax.axis_index("tensor")
    rows = local_rows.shape[0]
    pieces = [shift_by(local_rows, step) for step in range(1, size)]
    if size == 2:
        first = jnp.where(rank == 0, local_rows, pieces[0])
        second = jnp.where(rank == 0, pieces[0], local_rows)
        return jnp.concatenate([first, second], axis=0)
    whole = jnp.zeros((rows * size,) + local_rows.shape[1:], local_rows.dtype)
    whole = lax.dynamic_update_slice_in_dim(whole, local_rows, rank * rows, 0)
    for step, piece in enumerate(pieces, 1):
        whole = lax.dynamic_update_slice_in_dim(whole, piece, (rank - step) % size * rows, 0)
    return whole


def spread_product(left_side, product, rows):
    size = lax.axis_size("tensor")
    rank = lax.axis_index("tensor")

    def piece_for(owner):
        return product(lax.dynamic_slice_in_dim(left_side, owner * rows, rows, 0))

    arrived = [
        shift_by(piece_for((rank + step) % size).astype(jnp.bfloat16), step)
        for step in range(1, size)
    ]
    total = piece_for(rank)
    for piece in arrived:
        total = total + piece.astype(jnp.float32)
    return total


def sum_everywhere(vectors):
    sizes = [v.size for v in vectors]
    flat = jnp.concatenate([v.reshape(-1) for v in vectors]).reshape(-1, LANES)
    for axis in ("tensor", "dp"):
        size = lax.axis_size(axis)
        hop = 1
        while hop < size:
            flat = flat + lax.ppermute(flat, axis, [(i, i ^ hop) for i in range(size)])
            hop *= 2
    flat = flat.reshape(-1)
    out, start = [], 0
    for v, n in zip(vectors, sizes):
        out.append(flat[start : start + n].reshape(v.shape))
        start += n
    return out


def contract_rows(left_side, right_side):
    return lax.dot_general(
        left_side, right_side, (((0,), (0,)), ((), ())), preferred_element_type=jnp.float32
    )


def contract_cols(left_side, right_side):
    return lax.dot_general(
        left_side, right_side, (((1,), (1,)), ((), ())), preferred_element_type=jnp.float32
    )


def times(left_side, right_side):
    return jnp.dot(left_side, right_side, preferred_element_type=jnp.float32)


SCALE = 1.0 / math.sqrt(HD)


def only_head(values, head):
    lane = lax.broadcasted_iota(jnp.int32, values.shape, 1)
    return jnp.where(lane // HD == head, values, jnp.zeros_like(values))


def causal_scores(query_block, keys, start):
    scores = contract_cols(query_block, keys) * SCALE
    row = lax.broadcasted_iota(jnp.int32, scores.shape, 0) + start
    col = lax.broadcasted_iota(jnp.int32, scores.shape, 1)
    return jnp.where(col <= row, scores, -1e30)


def forward_kernel(q_ref, k_ref, v_ref, o_ref, lse_ref):
    keys = [only_head(k_ref[...], head) for head in range(2)]
    values = [only_head(v_ref[...], head) for head in range(2)]
    lane = lax.broadcasted_iota(jnp.int32, (QB, LANES), 1)
    for block in range(LEN // QB):
        start, stop = block * QB, (block + 1) * QB
        query_block = q_ref[start:stop, :]
        attended = jnp.zeros((QB, LANES), jnp.float32)
        logs = []
        for head in range(2):
            scores = causal_scores(query_block, keys[head][:stop], start)
            top = jnp.max(scores, axis=-1, keepdims=True)
            weights = jnp.exp(scores - top)
            total = jnp.sum(weights, axis=-1, keepdims=True)
            weights = (weights * (1.0 / total)).astype(jnp.bfloat16)
            attended += times(weights, values[head][:stop])
            logs.append(top + jnp.log(total))
        o_ref[start:stop, :] = attended.astype(jnp.bfloat16)
        lse_ref[start:stop, :] = jnp.where(lane < HD, logs[0], logs[1])


def backward_kernel(q_ref, k_ref, v_ref, o_ref, do_ref, lse_ref, out_ref, dk_ref, dv_ref):
    pair = pl.program_id(1)
    width = out_ref.shape[1] // 3
    keys = [only_head(k_ref[...], head) for head in range(2)]
    values = [only_head(v_ref[...], head) for head in range(2)]
    dk_ref[...] = jnp.zeros_like(dk_ref)
    dv_ref[...] = jnp.zeros_like(dv_ref)

    def columns(part):
        return pl.ds(pl.multiple_of(part * width + pair * LANES, LANES), LANES)

    for block in range(LEN // QB):
        start, stop = block * QB, (block + 1) * QB
        query_block = q_ref[start:stop, :]
        d_block = do_ref[start:stop, :]
        both = d_block.astype(jnp.float32) * o_ref[start:stop, :].astype(jnp.float32)
        d_query = jnp.zeros((QB, LANES), jnp.float32)
        for head in range(2):
            scores = causal_scores(query_block, keys[head][:stop], start)
            weights = jnp.exp(scores - lse_ref[start:stop, head * HD : head * HD + 1])
            d_weights = contract_cols(d_block, values[head][:stop])
            delta = jnp.sum(only_head(both, head), axis=-1, keepdims=True)
            d_scores = (weights * (d_weights - delta)).astype(jnp.bfloat16)
            d_query += times(d_scores, keys[head][:stop])
            dk_ref[:stop, :] += contract_rows(d_scores, only_head(query_block, head))
            dv_ref[:stop, :] += contract_rows(
                weights.astype(jnp.bfloat16), only_head(d_block, head)
            )
        out_ref[start:stop, columns(0)] = (d_query * SCALE).astype(jnp.bfloat16)
    out_ref[:, columns(1)] = (dk_ref[...] * SCALE).astype(jnp.bfloat16)
    out_ref[:, columns(2)] = dv_ref[...].astype(jnp.bfloat16)


def pair_block(part, pairs):
    return pl.BlockSpec((LEN, LANES), lambda s, p: (s, part * pairs + p))


def attend_forward(qkv):
    rows, width = qkv.shape[0], qkv.shape[1] // 3
    pairs = width // LANES
    return pl.pallas_call(
        forward_kernel,
        grid=(rows // LEN, pairs),
        in_specs=[pair_block(part, pairs) for part in range(3)],
        out_specs=[pair_block(0, pairs), pair_block(0, pairs)],
        out_shape=[
            jax.ShapeDtypeStruct((rows, width), jnp.bfloat16),
            jax.ShapeDtypeStruct((rows, width), jnp.float32),
        ],
        compiler_params=pltpu.CompilerParams(vmem_limit_bytes=40 * 2**20),
        cost_estimate=pl.CostEstimate(
            flops=8 * rows * LEN * width, bytes_accessed=10 * rows * width, transcendentals=0
        ),
        name="attend_forward",
    )(qkv, qkv, qkv)


def attend_backward(qkv, attended, d_attended, log_totals):
    rows, width = qkv.shape[0], qkv.shape[1] // 3
    pairs = width // LANES
    return pl.pallas_call(
        backward_kernel,
        grid=(rows // LEN, pairs),
        in_specs=[pair_block(part, pairs) for part in range(3)] + [pair_block(0, pairs)] * 3,
        out_specs=pl.BlockSpec((LEN, 3 * width), lambda s, p: (s, 0)),
        out_shape=jax.ShapeDtypeStruct((rows, 3 * width), jnp.bfloat16),
        scratch_shapes=[pltpu.VMEM((LEN, LANES), jnp.float32)] * 2,
        compiler_params=pltpu.CompilerParams(vmem_limit_bytes=40 * 2**20),
        cost_estimate=pl.CostEstimate(
            flops=20 * rows * LEN * width, bytes_accessed=20 * rows * width, transcendentals=0
        ),
        name="attend_backward",
    )(qkv, qkv, qkv, attended, d_attended, log_totals)


def over_dp(shard):
    return lax.all_gather(shard, "dp", axis=0, tiled=True)


def shard_over_dp(grad):
    return lax.psum_scatter(grad, "dp", scatter_dimension=0, tiled=True)


def body(
    tokens,
    ln1_gain,
    ln1_bias,
    w_qkv,
    qv_bias,
    w_out,
    out_bias,
    ln2_gain,
    ln2_bias,
    w_fc,
    fc_bias,
    w_proj,
    proj_bias,
    cotangent,
):
    tok_rows = tokens.shape[0]
    tensor_rank = lax.axis_index("tensor")
    head_cols = w_qkv.shape[2]
    hidden_cols = w_fc.shape[1]
    attn_shard = jnp.concatenate([w_qkv[0], w_qkv[1], w_qkv[2], w_out.T], axis=1)
    attn_full = over_dp(attn_shard)
    qkv_full = attn_full[:, : 3 * head_cols]
    out_cols = attn_full[:, 3 * head_cols :]
    fc_full = over_dp(w_fc)
    proj_full = over_dp(w_proj.T)

    bias_qv = lax.dynamic_slice_in_dim(qv_bias, tensor_rank * head_cols, head_cols, 1)
    bias_qkv = jnp.concatenate([bias_qv[0], jnp.zeros_like(bias_qv[0]), bias_qv[1]])
    inputs = tokens.astype(jnp.float32)
    normed_one, norm_one_back = jax.vjp(norm_rows, inputs, ln1_gain, ln1_bias)
    seen_one = gather_rows(normed_one.astype(jnp.bfloat16))
    seen_grad = gather_rows(cotangent)
    qkv = (times(seen_one, qkv_full) + bias_qkv).astype(jnp.bfloat16)
    attended, log_totals = attend_forward(qkv)
    branch_one = spread_product(attended, lambda piece: contract_cols(piece, out_cols), tok_rows)
    hidden_res = inputs + (branch_one + out_bias)
    normed_two, norm_two_back = jax.vjp(norm_rows, hidden_res, ln2_gain, ln2_bias)
    seen_two = gather_rows(normed_two.astype(jnp.bfloat16))
    bias_hidden = lax.dynamic_slice_in_dim(fc_bias, tensor_rank * hidden_cols, hidden_cols, 0)
    pre_act = times(seen_two, fc_full) + bias_hidden
    activated, gelu_back = jax.vjp(gelu_tanh, pre_act)
    activated = activated.astype(jnp.bfloat16)
    d_pre = gelu_back(times(seen_grad, proj_full))[0].astype(jnp.bfloat16)
    d_normed_two = spread_product(d_pre, lambda piece: contract_cols(piece, fc_full), tok_rows)
    grad_proj = shard_over_dp(contract_rows(seen_grad, activated).astype(jnp.bfloat16))
    branch_two = spread_product(activated, lambda piece: contract_cols(piece, proj_full), tok_rows)
    block_out = (hidden_res + (branch_two + proj_bias)).astype(jnp.bfloat16)
    grad_fc = shard_over_dp(contract_rows(seen_two, d_pre).astype(jnp.bfloat16))

    grad_final = cotangent.astype(jnp.float32)
    grad_proj_bias = jnp.sum(grad_final, axis=0)
    local_bias_grad = jnp.sum(d_pre, axis=0, dtype=jnp.float32)
    grad_fc_bias = lax.dynamic_update_slice_in_dim(
        jnp.zeros(fc_bias.shape, jnp.float32), local_bias_grad, tensor_rank * hidden_cols, 0
    )
    d_hidden_norm, grad_ln2_gain, grad_ln2_bias = norm_two_back(d_normed_two)
    grad_hidden = grad_final + d_hidden_norm
    grad_hidden_low = grad_hidden.astype(jnp.bfloat16)
    grad_out_bias = jnp.sum(grad_hidden_low, axis=0, dtype=jnp.float32)
    seen_hidden = gather_rows(grad_hidden_low)
    d_attended = times(seen_hidden, out_cols).astype(jnp.bfloat16)
    early = sum_everywhere(
        [grad_out_bias, grad_ln2_gain, grad_ln2_bias, grad_fc_bias, grad_proj_bias]
    )
    d_qkv_rows = attend_backward(qkv, attended, d_attended, log_totals)
    d_normed_one = spread_product(
        d_qkv_rows, lambda piece: contract_cols(piece, qkv_full), tok_rows
    )
    grad_attn = shard_over_dp(
        jnp.concatenate(
            [
                contract_rows(seen_one, d_qkv_rows).astype(jnp.bfloat16),
                contract_rows(seen_hidden, attended).astype(jnp.bfloat16),
            ],
            axis=1,
        )
    ).astype(jnp.float32)
    bias_sums = jnp.sum(d_qkv_rows, axis=0, dtype=jnp.float32)
    local_qv = jnp.stack([bias_sums[:head_cols], bias_sums[2 * head_cols :]])
    grad_qv_bias = lax.dynamic_update_slice_in_dim(
        jnp.zeros(qv_bias.shape, jnp.float32), local_qv, tensor_rank * head_cols, 1
    )
    d_inputs_norm, grad_ln1_gain, grad_ln1_bias = norm_one_back(d_normed_one)
    input_grad = (grad_hidden + d_inputs_norm).astype(jnp.bfloat16)
    late = sum_everywhere([grad_ln1_gain, grad_ln1_bias, grad_qv_bias])
    grad_qkv = jnp.stack(
        [grad_attn[:, part * head_cols : (part + 1) * head_cols] for part in range(3)]
    )
    return (
        block_out,
        input_grad,
        late[0],
        late[1],
        grad_qkv,
        late[2],
        grad_attn[:, 3 * head_cols :].T,
        early[0],
        early[1],
        early[2],
        grad_fc.astype(jnp.float32),
        early[3],
        grad_proj.astype(jnp.float32).T,
        early[4],
    )


def solution(mesh):
    in_specs = (
        P(("dp", "tensor"), None),
        P(),
        P(),
        P(None, "dp", "tensor"),
        P(),
        P("tensor", "dp"),
        P(),
        P(),
        P(),
        P("dp", "tensor"),
        P(),
        P("tensor", "dp"),
        P(),
        P(("dp", "tensor"), None),
    )
    out_specs = (
        P(("dp", "tensor"), None),
        P(("dp", "tensor"), None),
        P(),
        P(),
        P(None, "dp", "tensor"),
        P(),
        P("tensor", "dp"),
        P(),
        P(),
        P(),
        P("dp", "tensor"),
        P(),
        P("tensor", "dp"),
        P(),
    )
    return jax.shard_map(body, mesh=mesh, in_specs=in_specs, out_specs=out_specs, check_vma=False)
```

time: 987 us -> 432 us (0.44)
  waiting for transfers between devices: 634 us -> 235 us
  matrix products: 177 us -> 81.5 us
  blocking collectives: 40.8 us -> 0 us
  other arithmetic: 67.1 us -> 28.9 us
  Pallas kernels: 0 us -> 34.2 us
  local copies, waits for them, and re-layouts: 32.7 us -> 9.42 us
  starting transfers between devices: 1.23 us -> 22.3 us
  loops' own time: 13.8 us -> 0 us
    all_gather x8 -> x3, waiting for transfers between devices: 251 us -> 23.3 us  [over_dp(): return lax.all_gather(shard, 'dp', axis=0, tiled=True)]
    reduce_scatter x7 -> x3, waiting for transfers between devices: 266 us -> 61.1 us  [shard_over_dp(): return lax.psum_scatter(grad, 'dp', scatter_dimension=0, tiled=True)]
    ppermute x0 -> x18, waiting for transfers between devices: none -> 149 us  [the longest x8 139 us: shift_by(): lax.ppermute(values, 'tensor', [(i, (i + step) % size) for i in range(siz...]
    unnamed x17 -> x6, waiting for transfers between devices: 116 us -> 1.44 us
    dot_general x20 -> x4, matrix products: 129 us -> 35.7 us  [times(): return jnp.dot(left_side, right_side, preferred_element_type=jnp.float32)]
    psum x1 -> x0, blocking collectives: 40.8 us -> none  [body(): lax.psum((grad_ln1_gain, grad_ln1_bias, grad_qv_bias, grad_out_bias, grad...]
    pallas_call x0 -> x2, Pallas kernels: none -> 34.2 us  [the longest x1 20.1 us: attend_backward(): pl.pallas_call(backward_kernel, grid=(rows // LEN, pairs), in_specs=[pair...]
    convert_element_type x9 -> x3, other arithmetic: 29.3 us -> 4.14 us  [the longest x1 1.79 us: body(): grad_fc.astype(jnp.float32)]
  transfers between devices with their start and end apart: 16 -> 24, of which waited for: 14 -> 14; matrix products, arithmetic and copies ran while one was open for 23% -> 21% of each run, Pallas kernels for 0% -> 8%
where the time goes in v1:
time: 432 us; the launch traced here: 426 us
  waiting for transfers between devices  235 us (54%)
  matrix products  81.5 us (19%)
  Pallas kernels  34.2 us (8%)
  other arithmetic  28.9 us (7%)
  starting transfers between devices  22.3 us (5%)
  between operations  14.9 us (3%)
  local copies, waits for them, and re-layouts  9.42 us (2%)
    ppermute x8, waiting for transfers between devices, shift_by(): lax.ppermute(values, 'tensor', [(i, (i + step) % size) for i in range(siz...  139 us
    reduce_scatter x3, waiting for transfers between devices, shard_over_dp(): return lax.psum_scatter(grad, 'dp', scatter_dimension=0, tiled=True)  61.1 us
    dot_general x4, matrix products, times(): return jnp.dot(left_side, right_side, preferred_element_type=jnp.float32)  35.7 us
    dot_general x8, matrix products, contract_cols(): lax.dot_general(left_side, right_side, (((1,), (1,)), ((), ())), preferre...  28 us
    all_gather x3, waiting for transfers between devices, over_dp(): return lax.all_gather(shard, 'dp', axis=0, tiled=True)  23.3 us
    pallas_call x1, Pallas kernels, attend_backward(): pl.pallas_call(backward_kernel, grid=(rows // LEN, pairs), in_specs=[pair...  20.1 us
    dot_general x4, matrix products, contract_rows(): lax.dot_general(left_side, right_side, (((0,), (0,)), ((), ())), preferre...  17.8 us
    pallas_call x1, Pallas kernels, attend_forward(): pl.pallas_call(forward_kernel, grid=(rows // LEN, pairs), in_specs=[pair_...  14.1 us
  transfers between devices with their start and end apart: 24, of which 14 were waited for; matrix products, arithmetic and copies ran while one was open for 21% of the time, Pallas kernels for 8%

profile of v1, /device:TPU:0, one launch (start us, length us, event | category | flops | bytes accessed | tf_op | source)
XLA Modules:
  0.0 426.3 jit_solution(5742136657543506358)
XLA Ops:
  7.3 1.0 slice_bitcast_fusion.6
  8.3 1.6 pad_maximum_fusion.16
  9.9 0.7 all-gather.6.cloned.1.call-update
  12.5 3.1 collective-permute-start
  15.7 23.2 %collective-permute-done = bf16[512,1024]{1,0:T(8,128)(2,1)} collective-permute-done((bf16[512,1024]{1,0:T(8,128)(2,1)S(1)}, bf16[512,1024]{1,0:T(8,128)(2,1)}, u32[]{:S(2)}, u32[]{:S(2)}) %collective-permute-start) | collective-permute-done | bytes 1048608 | tf_op jit(solution)/shard_map/ppermute | solution.py:32
  38.8 1.9 broadcast_select_fusion.7
  40.8 23.3 %all-gather.4.cloned.1.call-done = bf16[1024,2048]{1,0:T(8,128)(2,1)} async-done(((bf16[64,2048]{1,0:T(8,128)(2,1)}), bf16[1024,2048]{1,0:T(8,128)(2,1)}) %all-gather.4.cloned.1.call-update) | async-done | bytes 4194320 | tf_op jit(solution)/shard_map/all_gather | solution.py:213
  64.1 6.3 %add_convert_fusion.q_ref.k_ref.v_ref = bf16[1024,1536]{1,0:T(8,128)(2,1)S(1)} fusion(f32[1536]{0:T(1024)S(1)} %pad_maximum_fusion.17, bf16[1024,2048]{1,0:T(8,128)(2,1)} %all-gather.4.cloned.1.call-done, bf16[512,1024]{1,0:T(8,128)(2,1)S(1)} %get-tuple-element.35, bf16[512,1024]{1,0:T(8,128)(2,1)S(1)} %get-tuple-element.34), kind=kOutput, calls=%fused_computation.12 | convolution fusion | flops 3228565504 | bytes 8394752 | tf_op jit(solution)/shard_map/dot_general | solution.py:98
  70.4 14.1 %attend_forward.1 = (bf16[1024,512]{1,0:T(8,128)(2,1)S(1)}, f32[1024,512]{1,0:T(8,128)S(1)}) custom-call(bf16[1024,1536]{1,0:T(8,128)(2,1)S(1)} %add_convert_fusion.q_ref.k_ref.v_ref, bf16[1024,1536]{1,0:T(8,128)(2,1)S(1)} %add_convert_fusion.q_ref.k_ref.v_ref, bf16[1024,1536]{1,0:T(8,128)(2,1)S(1)} %add_convert_fusion.q_ref.k_ref.v_ref), custom_call_target="tpu_custom_call" | custom-call | flops 4294967296 | bytes 5242880 | tf_op jit(solution)/shard_map/attend_forward/pallas_call | solution.py:177
  84.6 0.7 convolution_convert_fusion.5
  85.4 1.5 collective-permute-start.1
  87.5 24.0 %collective-permute-done.1 = bf16[512,1024]{1,0:T(8,128)(2,1)S(1)} collective-permute-done((bf16[512,1024]{1,0:T(8,128)(2,1)S(1)}, bf16[512,1024]{1,0:T(8,128)(2,1)S(1)}, u32[]{:S(2)}, u32[]{:S(2)}) %collective-permute-start.1) | collective-permute-done | bytes 1048608 | tf_op jit(solution)/shard_map/ppermute | solution.py:32
  111.4 1.0 fusion.86
  113.2 1.4 add_convert_fusion.3
  114.6 1.5 collective-permute-start.2
  116.1 17.9 %collective-permute-done.4 = bf16[512,1024]{1,0:T(8,128)(2,1)} collective-permute-done((bf16[512,1024]{1,0:T(8,128)(2,1)}, bf16[512,1024]{1,0:T(8,128)(2,1)}, u32[]{:S(2)}, u32[]{:S(2)}) %collective-permute-start.4) | collective-permute-done | bytes 1048608 | tf_op jit(solution)/shard_map/ppermute | solution.py:32
  134.0 3.0 broadcast_select_fusion.3
  137.0 18.8 %collective-permute-done.2 = bf16[512,1024]{1,0:T(8,128)(2,1)} collective-permute-done((bf16[512,1024]{1,0:T(8,128)(2,1)}, bf16[512,1024]{1,0:T(8,128)(2,1)}, u32[]{:S(2)}, u32[]{:S(2)}) %collective-permute-start.2) | collective-permute-done | bytes 1048608 | tf_op jit(solution)/shard_map/ppermute | solution.py:32
  155.8 3.2 broadcast_select_fusion.5
  159.0 13.4 %multiply_convert_fusion = (bf16[1024,2048]{1,0:T(8,128)(2,1)}, f32[1024,2048]{1,0:T(8,128)}) fusion(f32[2048]{0:T(1024)S(1)} %dynamic_slice.33, bf16[1024,2048]{1,0:T(8,128)(2,1)} %all-gather.6.cloned.1.call-done, bf16[512,1024]{1,0:T(8,128)(2,1)} %get-tuple-element.33, bf16[512,1024]{1,0:T(8,128)(2,1)} %get-tuple-element.32), kind=kOutput, calls=%fused_computation.10 | convolution fusion | flops 4320133120 | bytes 18882560 | tf_op jit(solution)/shard_map/dot_general | solution.py:98
  172.4 13.5 %convert_reduce_fusion = (f32[2048]{0:T(1024)S(1)}, bf16[1024,2048]{1,0:T(8,128)(2,1)S(1)}) fusion(f32[1024,2048]{1,0:T(8,128)} %get-tuple-element.58, f32[2048]{0:T(1024)S(1)} %dynamic_slice.33, bf16[1024,2048]{1,0:T(8,128)(2,1)} %all-gather.8.cloned.1.call-done, bf16[512,1024]{1,0:T(8,128)(2,1)} %get-tuple-element.31, bf16[512,1024]{1,0:T(8,128)(2,1)} %get-tuple-element.30), kind=kOutput, calls=%fused_computation.9 | convolution fusion | flops 4347394048 | bytes 18890752 | tf_op jit(solution)/shard_map/dot_general | solution.py:98
  186.0 2.0 copy-done.33
  187.9 6.3 %convolution_convert_fusion.2 = bf16[1024,2048]{1,0:T(8,128)(2,1)} fusion(bf16[1024,2048]{1,0:T(8,128)(2,1)S(1)} %get-tuple-element.63, bf16[512,1024]{1,0:T(8,128)(2,1)S(1)} %copy-done.20, bf16[512,1024]{1,0:T(8,128)(2,1)S(1)} %copy-done.19), kind=kOutput, calls=%fused_computation.16 | convolution fusion | flops 4301258752 | bytes 10485760 | tf_op jit(solution)/shard_map/dot_general | solution.py:86
  194.4 6.3 %fusion.42 = bf16[512,1024]{1,0:T(8,128)(2,1)} fusion(bf16[1024,2048]{1,0:T(8,128)(2,1)} %all-gather.6.cloned.1.call-done, bf16[1024,2048]{1,0:T(8,128)(2,1)} %copy-done.33, s32[]{:T(128)S(6)} %select_n.72), kind=kOutput, calls=%fused_computation.64 | convolution fusion | flops 2148007936 | bytes 7340036 | tf_op jit(solution)/shard_map/dot_general | solution.py:92
  200.7 1.5 collective-permute-start.5
  202.2 6.3 %convolution_convert_fusion.1 = bf16[1024,2048]{1,0:T(8,128)(2,1)} fusion(bf16[1024,2048]{1,0:T(8,128)(2,1)S(1)} %copy-done.34, bf16[512,1024]{1,0:T(8,128)(2,1)S(1)} %copy-done.18, bf16[512,1024]{1,0:T(8,128)(2,1)S(1)} %copy-done.17), kind=kOutput, calls=%fused_computation.15 | convolution fusion | flops 4301258752 | bytes 10485760 | tf_op jit(solution)/shard_map/dot_general | solution.py:86
  208.7 16.8 %collective-permute-done.5 = bf16[512,1024]{1,0:T(8,128)(2,1)} collective-permute-done((bf16[512,1024]{1,0:T(8,128)(2,1)}, bf16[512,1024]{1,0:T(8,128)(2,1)}, u32[]{:S(2)}, u32[]{:S(2)}) %collective-permute-start.5) | collective-permute-done | bytes 1048608 | tf_op jit(solution)/shard_map/ppermute | solution.py:32
  225.5 6.0 %multiply_reduce_fusion = (f32[1024]{0:T(1024)S(1)}, f32[512]{0:T(512)S(1)}, f32[1024]{0:T(1024)S(1)}, f32[512,1024]{1,0:T(8,128)S(1)}) fusion(f32[512,1024]{1,0:T(8,128)S(1)} %copy-done.9, f32[512]{0:T(512)S(1)} %fusion.72, f32[512]{0:T(512)S(1)} %broadcast_multiply_fusion, f32[1024]{0:T(1024)S(1)} %copy-done.22, ...), kind=kOutput, calls=%fused_computation.44 | convolution fusion | flops 2152723968 | bytes 11552772 | tf_op jit(solution)/shard_map/dot_general | solution.py:92
  231.6 0.7 fusion.84
  232.3 2.8 convert_reduce_fusion.4
  235.1 1.5 collective-permute-start.6
  236.6 3.4 fusion.39
  240.0 1.0 collective-permute-start.3
  241.2 20.0 %collective-permute-done.6 = bf16[512,1024]{1,0:T(8,128)(2,1)S(1)} collective-permute-done((bf16[512,1024]{1,0:T(8,128)(2,1)S(1)}, bf16[512,1024]{1,0:T(8,128)(2,1)S(1)}, u32[]{:S(2)}, u32[]{:S(2)}) %collective-permute-start.6) | collective-permute-done | bytes 1048608 | tf_op jit(solution)/shard_map/ppermute | solution.py:32
  261.4 2.5 convolution_convert_fusion.4.do_ref
  263.9 1.3 convolution_convert_fusion.3
  266.4 1.2 copy-done.1
  267.7 20.1 %attend_backward.1 = bf16[1024,1536]{1,0:T(8,128)(2,1)S(1)} custom-call(bf16[1024,1536]{1,0:T(8,128)(2,1)S(1)} %copy-done.3, bf16[1024,1536]{1,0:T(8,128)(2,1)S(1)} %copy-done.3, bf16[1024,1536]{1,0:T(8,128)(2,1)S(1)} %copy-done.3, bf16[1024,512]{1,0:T(8,128)(2,1)S(1)} %copy-done.1, bf16[1024,512]{1,0:T(8,128)(2,1)S(1)} %convolution_convert_fusion.4.do_ref, ...), custom_call_target="tpu_custom_call" | custom-call | flops 10737418240 | bytes 10485760 | tf_op jit(solution)/shard_map/attend_backward/pallas_call | solution.py:197
  287.8 3.9 convolution_convert_fusion
  291.7 2.6 pad_maximum_fusion
  294.4 3.9 fusion.45
  298.2 1.5 collective-permute-start.7
  300.3 18.2 %collective-permute-done.7 = bf16[512,1024]{1,0:T(8,128)(2,1)S(1)} collective-permute-done((bf16[512,1024]{1,0:T(8,128)(2,1)S(1)}, bf16[512,1024]{1,0:T(8,128)(2,1)S(1)}, u32[]{:S(2)}, u32[]{:S(2)}) %collective-permute-start.7) | collective-permute-done | bytes 1048608 | tf_op jit(solution)/shard_map/ppermute | solution.py:32
  318.5 2.1 fusion.22
  320.7 1.0 fusion.20
  321.7 1.6 collective-permute-start.8
  323.3 3.2 convert_reduce_fusion.3
  327.1 3.3 collective-permute-done.13
  330.4 0.8 collective-permute-start.10
  331.6 1.0 collective-permute-start.15
  332.6 1.6 collective-permute-done.10
  334.2 1.7 collective-permute-start.11
  335.9 2.8 collective-permute-done.11
  338.7 1.4 collective-permute-start.12
  340.1 1.3 collective-permute-start.16
  341.3 4.7 %add_convert_fusion.2 = bf16[512,1024]{1,0:T(8,128)(2,1)} fusion(f32[512,1024]{1,0:T(8,128)S(1)} %copy-done.10, bf16[512,1024]{1,0:T(8,128)(2,1)} %collective-permute-done.3, bf16[1024,2048]{1,0:T(8,128)(2,1)S(1)} %copy-done.28, bf16[1024,2048]{1,0:T(8,128)(2,1)S(1)} %copy-done.36, s32[]{:T(128)S(6)} %select_n.70, f32[1024]{0:T(1024)S(1)} %copy-done.32), kind=kOutput, calls=%fused_computation.54 | convolution fusion | flops 2150105088 | bytes 10489860 | tf_op jit(solution)/shard_map/dot_general | solution.py:92
  346.0 1.5 collective-permute-start.17
  348.7 2.2 collective-permute-done.17
  352.2 1.8 convert_element_type.111
  353.9 1.8 convert_bitcast_fusion
  355.7 61.1 %reduce-scatter.4.cloned.1.call-done = bf16[64,2048]{1,0:T(8,128)(2,1)} async-done(((bf16[1024,2048]{1,0:T(8,128)(2,1)}), bf16[64,2048]{1,0:T(8,128)(2,1)}) %reduce-scatter.4.cloned.1.call-update) | async-done | bytes 262160 | tf_op jit(solution)/shard_map/reduce_scatter | solution.py:217
  416.8 1.0 convert_element_type.107
  417.8 0.7 slice_bitcast_fusion
  418.5 0.8 pad_maximum_fusion.15
  (143 shorter events, 9.5 us)
Async XLA Ops:
  7.2 4.2 copy-start.6
  7.2 4.9 %copy-start.21 = (f32[1024]{0:T(1024)S(1)}, f32[1024]{0:T(1024)}, u32[]{:S(2)}) copy-start(f32[1024]{0:T(1024)} %param.15) | copy-start | bytes 12292
  7.2 4.9 %copy-start.23 = (f32[1024]{0:T(1024)S(1)}, f32[1024]{0:T(1024)}, u32[]{:S(2)}) copy-start(f32[1024]{0:T(1024)} %param.16) | copy-start | bytes 12292
  7.2 56.9 %all-gather.4.cloned.1.call-start = ((), (), s32[]{:S(2)}) async-start(), calls=%async_computation.3 | async-start | bytes 4456448 | tf_op jit(solution)/shard_map/all_gather | solution.py:213
  9.8 149.2 %all-gather.6.cloned.1.call-start = ((), (), s32[]{:S(2)}) async-start(), calls=%async_computation.4 | async-start | bytes 4456448 | tf_op jit(solution)/shard_map/all_gather | solution.py:213
  10.6 161.8 %all-gather.8.cloned.1.call-start = ((), (), s32[]{:S(2)}) async-start(), calls=%async_computation.5 | async-start | bytes 4456448 | tf_op jit(solution)/shard_map/all_gather | solution.py:213
  11.3 4.2 copy-start.26
  11.3 340.8 %reduce-scatter.6.cloned.1.call-start = ((), (), s32[]{:S(2)}) async-start(), calls=%async_computation.7 | async-start | bytes 4456448 | tf_op jit(solution)/shard_map/reduce_scatter | solution.py:217
  12.5 26.3 %collective-permute-start = (bf16[512,1024]{1,0:T(8,128)(2,1)S(1)}, bf16[512,1024]{1,0:T(8,128)(2,1)}, u32[]{:S(2)}, u32[]{:S(2)}) collective-permute-start(bf16[512,1024]{1,0:T(8,128)(2,1)S(1)} %fusion.19), channel_id=1, source_target_pairs={{0,1},{1,0},{2,3},{3,2},{4,5},{5,4},{6,7},{7,6},{8,9},{9,8},{10,11... | collective-permute-start | bytes 3145736 | tf_op jit(solution)/shard_map/ppermute | solution.py:32
  40.8 23.3 %copy-start.13 = (bf16[512,1024]{1,0:T(8,128)(2,1)}, bf16[512,1024]{1,0:T(8,128)(2,1)S(1)}, u32[]{:S(2)}) copy-start(bf16[512,1024]{1,0:T(8,128)(2,1)S(1)} %get-tuple-element.34) | copy-start | bytes 3145732
  40.8 29.6 %copy-start.15 = (bf16[512,1024]{1,0:T(8,128)(2,1)}, bf16[512,1024]{1,0:T(8,128)(2,1)S(1)}, u32[]{:S(2)}) copy-start(bf16[512,1024]{1,0:T(8,128)(2,1)S(1)} %get-tuple-element.35) | copy-start | bytes 3145732
  70.4 14.2 %copy-start.2 = (bf16[1024,1536]{1,0:T(8,128)(2,1)}, bf16[1024,1536]{1,0:T(8,128)(2,1)S(1)}, u32[]{:S(2)}) copy-start(bf16[1024,1536]{1,0:T(8,128)(2,1)S(1)} %add_convert_fusion.q_ref.k_ref.v_ref) | copy-start | bytes 9437188
  70.4 14.2 %copy-start.29 = (bf16[1024,2048]{1,0:T(8,128)(2,1)S(1)}, bf16[1024,2048]{1,0:T(8,128)(2,1)}, u32[]{:S(2)}) copy-start(bf16[1024,2048]{1,0:T(8,128)(2,1)} %all-gather.4.cloned.1.call-done) | copy-start | bytes 12582916
  84.6 27.8 %copy-start.4 = (f32[1024,512]{1,0:T(8,128)}, f32[1024,512]{1,0:T(8,128)S(1)}, u32[]{:S(2)}) copy-start(f32[1024,512]{1,0:T(8,128)S(1)} %get-tuple-element.17.lse_ref) | copy-start | bytes 6291460
  84.6 179.3 %copy-start = (bf16[1024,512]{1,0:T(8,128)(2,1)}, bf16[1024,512]{1,0:T(8,128)(2,1)S(1)}, u32[]{:S(2)}) copy-start(bf16[1024,512]{1,0:T(8,128)(2,1)S(1)} %get-tuple-element.16.o_ref) | copy-start | bytes 3145732
  84.6 26.8 %copy-start.31 = (f32[1024]{0:T(1024)S(1)}, f32[1024]{0:T(1024)}, u32[]{:S(2)}) copy-start(f32[1024]{0:T(1024)} %param.20) | copy-start | bytes 12292
  85.4 26.1 %collective-permute-start.1 = (bf16[512,1024]{1,0:T(8,128)(2,1)S(1)}, bf16[512,1024]{1,0:T(8,128)(2,1)S(1)}, u32[]{:S(2)}, u32[]{:S(2)}) collective-permute-start(bf16[512,1024]{1,0:T(8,128)(2,1)S(1)} %convolution_convert_fusion.5), channel_id=1, source_target_pairs={{0,1},{1,0},{2,3},{3,2},{4,5},{5,4},{6,7},{7,6},{8,9},{9,8},{10,11... | collective-permute-start | bytes 3145736 | tf_op jit(solution)/shard_map/ppermute | solution.py:32
  86.9 47.1 %collective-permute-start.4 = (bf16[512,1024]{1,0:T(8,128)(2,1)}, bf16[512,1024]{1,0:T(8,128)(2,1)}, u32[]{:S(2)}, u32[]{:S(2)}) collective-permute-start(bf16[512,1024]{1,0:T(8,128)(2,1)} %param.27), channel_id=1, source_target_pairs={{0,1},{1,0},{2,3},{3,2},{4,5},{5,4},{6,7},{7,6},{8,9},{9,8},{10,11... | collective-permute-start | bytes 3145736 | tf_op jit(solution)/shard_map/ppermute | solution.py:32
  112.4 2.2 copy-start.8
  112.4 0.7 copy-start.22
  112.4 0.8 copy-start.24
  112.8 3.3 copy-start.25
  114.6 41.2 %collective-permute-start.2 = (bf16[512,1024]{1,0:T(8,128)(2,1)}, bf16[512,1024]{1,0:T(8,128)(2,1)}, u32[]{:S(2)}, u32[]{:S(2)}) collective-permute-start(bf16[512,1024]{1,0:T(8,128)(2,1)} %add_convert_fusion.3), channel_id=1, source_target_pairs={{0,1},{1,0},{2,3},{3,2},{4,5},{5,4},{6,7},{7,6},{8,9},{9,8},{10,11... | collective-permute-start | bytes 3145736 | tf_op jit(solution)/shard_map/ppermute | solution.py:32
  116.1 39.7 %copy-start.9 = (f32[512,1024]{1,0:T(8,128)S(1)}, f32[512,1024]{1,0:T(8,128)}, u32[]{:S(2)}) copy-start(f32[512,1024]{1,0:T(8,128)} %copy-done.8) | copy-start | bytes 6291460
  172.4 15.5 %copy-start.19 = (bf16[512,1024]{1,0:T(8,128)(2,1)S(1)}, bf16[512,1024]{1,0:T(8,128)(2,1)}, u32[]{:S(2)}) copy-start(bf16[512,1024]{1,0:T(8,128)(2,1)} %get-tuple-element.32) | copy-start | bytes 3145732
  172.4 15.5 %copy-start.20 = (bf16[512,1024]{1,0:T(8,128)(2,1)S(1)}, bf16[512,1024]{1,0:T(8,128)(2,1)}, u32[]{:S(2)}) copy-start(bf16[512,1024]{1,0:T(8,128)(2,1)} %get-tuple-element.33) | copy-start | bytes 3145732
  186.0 2.0 copy-start.33
  194.3 159.7 %reduce-scatter.8.cloned.1.call-start = ((), (), s32[]{:S(2)}) async-start(), calls=%async_computation.8 | async-start | bytes 4456448 | tf_op jit(solution)/shard_map/reduce_scatter | solution.py:217
  194.3 7.8 %copy-start.17 = (bf16[512,1024]{1,0:T(8,128)(2,1)S(1)}, bf16[512,1024]{1,0:T(8,128)(2,1)}, u32[]{:S(2)}) copy-start(bf16[512,1024]{1,0:T(8,128)(2,1)} %get-tuple-element.30) | copy-start | bytes 3145732
  194.3 7.8 %copy-start.18 = (bf16[512,1024]{1,0:T(8,128)(2,1)S(1)}, bf16[512,1024]{1,0:T(8,128)(2,1)}, u32[]{:S(2)}) copy-start(bf16[512,1024]{1,0:T(8,128)(2,1)} %get-tuple-element.31) | copy-start | bytes 3145732
  194.3 7.8 %copy-start.34 = (bf16[1024,2048]{1,0:T(8,128)(2,1)S(1)}, bf16[1024,2048]{1,0:T(8,128)(2,1)}, u32[]{:S(2)}) copy-start(bf16[1024,2048]{1,0:T(8,128)(2,1)} %get-tuple-element.57) | copy-start | bytes 12582916
  200.7 24.8 %collective-permute-start.5 = (bf16[512,1024]{1,0:T(8,128)(2,1)}, bf16[512,1024]{1,0:T(8,128)(2,1)}, u32[]{:S(2)}, u32[]{:S(2)}) collective-permute-start(bf16[512,1024]{1,0:T(8,128)(2,1)} %fusion.42), channel_id=1, source_target_pairs={{0,1},{1,0},{2,3},{3,2},{4,5},{5,4},{6,7},{7,6},{8,9},{9,8},{10,11... | collective-permute-start | bytes 3145736 | tf_op jit(solution)/shard_map/ppermute | solution.py:32
  208.5 208.4 %reduce-scatter.4.cloned.1.call-start = ((), (), s32[]{:S(2)}) async-start(), calls=%async_computation.6 | async-start | bytes 4456448 | tf_op jit(solution)/shard_map/reduce_scatter | solution.py:217
  231.5 5.1 %copy-start.35 = (bf16[1024,2048]{1,0:T(8,128)(2,1)S(1)}, bf16[1024,2048]{1,0:T(8,128)(2,1)}, u32[]{:S(2)}) copy-start(bf16[1024,2048]{1,0:T(8,128)(2,1)} %get-tuple-element.57) | copy-start | bytes 12582916
  232.3 2.8 copy-start.11
  232.3 4.3 %copy-start.27 = (bf16[1024,2048]{1,0:T(8,128)(2,1)S(1)}, bf16[1024,2048]{1,0:T(8,128)(2,1)}, u32[]{:S(2)}) copy-start(bf16[1024,2048]{1,0:T(8,128)(2,1)} %all-gather.8.cloned.1.call-done) | copy-start | bytes 12582916
  235.1 26.2 %collective-permute-start.6 = (bf16[512,1024]{1,0:T(8,128)(2,1)S(1)}, bf16[512,1024]{1,0:T(8,128)(2,1)S(1)}, u32[]{:S(2)}, u32[]{:S(2)}) collective-permute-start(bf16[512,1024]{1,0:T(8,128)(2,1)S(1)} %get-tuple-element.25), channel_id=1, source_target_pairs={{0,1},{1,0},{2,3},{3,2},{4,5},{5,4},{6,7},{7,6},{8,9},{9,8},{10,11... | collective-permute-start | bytes 3145736 | tf_op jit(solution)/shard_map/ppermute | solution.py:32
  240.0 101.4 %collective-permute-start.3 = (bf16[512,1024]{1,0:T(8,128)(2,1)}, bf16[512,1024]{1,0:T(8,128)(2,1)}, u32[]{:S(2)}, u32[]{:S(2)}) collective-permute-start(bf16[512,1024]{1,0:T(8,128)(2,1)} %fusion.39), channel_id=1, source_target_pairs={{0,1},{1,0},{2,3},{3,2},{4,5},{5,4},{6,7},{7,6},{8,9},{9,8},{10,11... | collective-permute-start | bytes 3145736 | tf_op jit(solution)/shard_map/ppermute | solution.py:32
  263.9 1.9 copy-start.3
  263.9 2.6 copy-start.5
  266.4 1.2 copy-start.1
  267.7 20.1 %copy-start.14 = (bf16[512,1024]{1,0:T(8,128)(2,1)S(1)}, bf16[512,1024]{1,0:T(8,128)(2,1)}, u32[]{:S(2)}) copy-start(bf16[512,1024]{1,0:T(8,128)(2,1)} %copy-done.13) | copy-start | bytes 3145732
  267.7 20.1 %copy-start.16 = (bf16[512,1024]{1,0:T(8,128)(2,1)S(1)}, bf16[512,1024]{1,0:T(8,128)(2,1)}, u32[]{:S(2)}) copy-start(bf16[512,1024]{1,0:T(8,128)(2,1)} %copy-done.15) | copy-start | bytes 3145732
  294.4 24.2 %copy-start.30 = (bf16[1024,2048]{1,0:T(8,128)(2,1)S(1)}, bf16[1024,2048]{1,0:T(8,128)(2,1)}, u32[]{:S(2)}) copy-start(bf16[1024,2048]{1,0:T(8,128)(2,1)} %all-gather.4.cloned.1.call-done) | copy-start | bytes 12582916
  298.2 20.3 %copy-start.7 = (bf16[512,1024]{1,0:T(8,128)(2,1)S(1)}, bf16[512,1024]{1,0:T(8,128)(2,1)}, u32[]{:S(2)}) copy-start(bf16[512,1024]{1,0:T(8,128)(2,1)} %param.14) | copy-start | bytes 3145732
  298.2 20.3 %collective-permute-start.7 = (bf16[512,1024]{1,0:T(8,128)(2,1)S(1)}, bf16[512,1024]{1,0:T(8,128)(2,1)S(1)}, u32[]{:S(2)}, u32[]{:S(2)}) collective-permute-start(bf16[512,1024]{1,0:T(8,128)(2,1)S(1)} %fusion.45), channel_id=1, source_target_pairs={{0,1},{1,0},{2,3},{3,2},{4,5},{5,4},{6,7},{7,6},{8,9},{9,8},{10,11... | collective-permute-start | bytes 3145736 | tf_op jit(solution)/shard_map/ppermute | solution.py:32
  318.5 22.8 %copy-start.36 = (bf16[1024,2048]{1,0:T(8,128)(2,1)S(1)}, bf16[1024,2048]{1,0:T(8,128)(2,1)}, u32[]{:S(2)}) copy-start(bf16[1024,2048]{1,0:T(8,128)(2,1)} %get-tuple-element.57) | copy-start | bytes 12582916
  320.6 2.6 copy-start.12
  321.7 5.3 %collective-permute-start.8 = (f32[32,128]{1,0:T(8,128)S(1)}, f32[32,128]{1,0:T(8,128)S(1)}, u32[]{:S(2)}, u32[]{:S(2)}) collective-permute-start(f32[32,128]{1,0:T(8,128)S(1)} %maximum_bitcast_fusion), channel_id=1, source_target_pairs={{0,1},{1,0},{2,3},{3,2},{4,5},{5,4},{6,7},{7,6},{8,9},{9,8},{10,11... | collective-permute-start | bytes 49160 | tf_op jit(solution)/shard_map/ppermute | solution.py:75
  323.3 18.0 %copy-start.10 = (f32[512,1024]{1,0:T(8,128)S(1)}, f32[512,1024]{1,0:T(8,128)}, u32[]{:S(2)}) copy-start(f32[512,1024]{1,0:T(8,128)} %copy-done.8) | copy-start | bytes 6291460
  323.3 18.0 %copy-start.28 = (bf16[1024,2048]{1,0:T(8,128)(2,1)S(1)}, bf16[1024,2048]{1,0:T(8,128)(2,1)}, u32[]{:S(2)}) copy-start(bf16[1024,2048]{1,0:T(8,128)(2,1)} %all-gather.8.cloned.1.call-done) | copy-start | bytes 12582916
  323.3 18.1 %copy-start.32 = (f32[1024]{0:T(1024)S(1)}, f32[1024]{0:T(1024)}, u32[]{:S(2)}) copy-start(f32[1024]{0:T(1024)} %param.26) | copy-start | bytes 12292
  326.5 3.9 collective-permute-start.13
  327.0 3.4 collective-permute-start.9
  330.4 1.2 collective-permute-start.14
  330.4 3.8 collective-permute-start.10
  331.6 8.5 %collective-permute-start.15 = (f32[64,128]{1,0:T(8,128)S(1)}, f32[64,128]{1,0:T(8,128)S(1)}, u32[]{:S(2)}, u32[]{:S(2)}) collective-permute-start(f32[64,128]{1,0:T(8,128)S(1)} %fusion.97), channel_id=1, source_target_pairs={{0,4},{2,6},{4,0},{6,2},{8,12},{10,14},{12,8},{14,10},{16,20},{18,... | collective-permute-start | bytes 98312 | tf_op jit(solution)/shard_map/ppermute | solution.py:75
  334.2 4.5 %collective-permute-start.11 = (f32[32,128]{1,0:T(8,128)S(1)}, f32[32,128]{1,0:T(8,128)S(1)}, u32[]{:S(2)}, u32[]{:S(2)}) collective-permute-start(f32[32,128]{1,0:T(8,128)S(1)} %add.197), channel_id=1, source_target_pairs={{0,8},{2,10},{4,12},{6,14},{8,0},{10,2},{12,4},{14,6},{16,24},{18,... | collective-permute-start | bytes 49160 | tf_op jit(solution)/shard_map/ppermute | solution.py:75
  338.7 7.3 %collective-permute-start.12 = (f32[32,128]{1,0:T(8,128)S(1)}, f32[32,128]{1,0:T(8,128)S(1)}, u32[]{:S(2)}, u32[]{:S(2)}) collective-permute-start(f32[32,128]{1,0:T(8,128)S(1)} %add.198), channel_id=1, source_target_pairs={{0,16},{2,18},{4,20},{6,22},{8,24},{10,26},{12,28},{14,30},{16,0},... | collective-permute-start | bytes 49160 | tf_op jit(solution)/shard_map/ppermute | solution.py:75
  340.1 6.0 %collective-permute-start.16 = (f32[64,128]{1,0:T(8,128)S(1)}, f32[64,128]{1,0:T(8,128)S(1)}, u32[]{:S(2)}, u32[]{:S(2)}) collective-permute-start(f32[64,128]{1,0:T(8,128)S(1)} %add.202), channel_id=1, source_target_pairs={{0,8},{2,10},{4,12},{6,14},{8,0},{10,2},{12,4},{14,6},{16,24},{18,... | collective-permute-start | bytes 98312 | tf_op jit(solution)/shard_map/ppermute | solution.py:75
  346.0 4.9 %collective-permute-start.17 = (f32[64,128]{1,0:T(8,128)S(1)}, f32[64,128]{1,0:T(8,128)S(1)}, u32[]{:S(2)}, u32[]{:S(2)}) collective-permute-start(f32[64,128]{1,0:T(8,128)S(1)} %add.203), channel_id=1, source_target_pairs={{0,16},{2,18},{4,20},{6,22},{8,24},{10,26},{12,28},{14,30},{16,0},... | collective-permute-start | bytes 98312 | tf_op jit(solution)/shard_map/ppermute | solution.py:75
Sparse Core Ops, SparseCore 0:
  10.8 53.2 all-gather.3
  66.2 49.2 all-gather.5
  117.6 49.0 all-gather.7
  194.4 70.8 reduce-scatter.5
  269.5 72.2 reduce-scatter.7
  345.5 71.3 reduce-scatter.3
